TPU v7x, 256 devices: a whole 4x4x8 slice. The times are simulated.
256 devices in a mesh: ctx: 16 (over y_lo, z), tp: 8 (over x, core), role: 2 (over y_hi).
Axes of the slice: x: 4, y: 4 (y_hi: 2, y_lo: 2; y = y_hi * 2 + y_lo), z: 8, core: 2. Of those that a mesh axis runs over, the one named last changes fastest.
Arguments:
- token_ids: int32 [2, 2048], P('role', 'ctx'), may hold values from 0 to 65535
- embed_table: bfloat16 [65536, 7168], P(('ctx', 'role'), 'tp'), may hold values from -6 to 6
- latent_down: bfloat16 [7168, 576], P('tp'), may hold values from -0.0625 to 0.0625
- latent_gain: float32 [512], replicated, may hold values from 0.1 to 1.9
- prefill_query: bfloat16 [2048, 64, 576], P('ctx', 'tp'), may hold values from -120 to 120
- decode_query: bfloat16 [1024, 2, 64, 576], P(('ctx', 'tp')), may hold values from -120 to 120
- latent_cache: bfloat16 [1024, 512, 576], P(('ctx', 'tp')), may hold values from -6 to 6
- cache_length: int32 [1024], P(('ctx', 'tp')), may hold values from 1 to 512, as said below
- prompt_owner: int32 [2], replicated, may hold values from 0 to 15
Outputs:
- attended: bfloat16 [2, 2048, 32768], P('role', 'ctx', 'tp')
Inputs may be any that keep to these rules, and one draw needn't show every extreme that they name: `cache_length`: some row has exactly 512.
All inputs are finite; a program needn't handle non-finite values.
Results may differ from a plain program's by a relative error of at most 0.0099.
Values may be sent and summed in bfloat16 or wider, within the bound.
No kernel may reach another device: no remote copies, remote signals or barrier semaphores. Data moves between devices by JAX's collectives and lax.ppermute only.
A program may use at most 128 MiB of HBM per device.

v0:
```python
import jax
import jax.numpy as jnp
from jax import lax
from jax.sharding import PartitionSpec as P

LAT = 512
STEPS = 2


score_scale = 0.07216878364870322
masked_fill = -1e30
norm_eps = 1e-06
rope_base = 10000.0


def passed_along(value, axis, steps):
    count = lax.axis_size(axis)
    leading, last = (max(0, -steps), min(count, count - steps))
    return lax.ppermute(value, axis, [(source, source + steps) for source in range(leading, last)])


def finish_keys(latent, latent_gain, position):
    plain = latent[:, :LAT]
    scaled = (
        plain * lax.rsqrt(jnp.mean(plain * plain, axis=-1, keepdims=True) + norm_eps) * latent_gain
    )
    rotary = latent[:, LAT:]
    half_width = rotary.shape[-1] // 2
    frequency = rope_base ** (-jnp.arange(half_width, dtype=jnp.float32) / half_width)
    angles = position.astype(jnp.float32)[:, None] * frequency[None, :]
    first_half = rotary[:, :half_width]
    second_half = rotary[:, half_width:]
    turned = jnp.concatenate(
        [
            first_half * jnp.cos(angles) - second_half * jnp.sin(angles),
            first_half * jnp.sin(angles) + second_half * jnp.cos(angles),
        ],
        axis=-1,
    )
    return jnp.concatenate([scaled, turned], axis=-1).astype(jnp.bfloat16)


def partial_part(scores, allowed, weigh_values):
    masked = jnp.where(allowed, scores, masked_fill)
    highest = jnp.max(masked, axis=-1)
    weights = jnp.where(allowed, jnp.exp(masked - highest[..., None]), 0.0)
    return (highest, jnp.sum(weights, axis=-1), weigh_values(weights.astype(jnp.bfloat16)))


def merge_parts(first_part, second_part):
    highest = jnp.maximum(first_part[0], second_part[0])
    factor_a = jnp.exp(first_part[0] - highest)
    factor_b = jnp.exp(second_part[0] - highest)
    return (
        highest,
        first_part[1] * factor_a + second_part[1] * factor_b,
        first_part[2] * factor_a[..., None] + second_part[2] * factor_b[..., None],
    )


def shards(
    token_ids,
    embed_table,
    latent_down,
    latent_gain,
    prefill_query,
    decode_query,
    latent_cache,
    cache_length,
    prompt_owner,
):
    role_count = lax.axis_size("role")
    section = lax.axis_index("role")
    group_index = lax.axis_index("ctx")
    tp_index = lax.axis_index("tp")
    block_rows = token_ids.shape[1]
    prompt_count = prompt_owner.shape[0]
    vocab_rows = embed_table.shape[0]
    offset = (group_index * role_count + section) * vocab_rows
    every_id = lax.all_gather(token_ids, ("ctx", "role"), axis=0, tiled=True)
    local_row = every_id.reshape(-1) - offset
    inside = (local_row >= 0) & (local_row < vocab_rows)
    picked = jnp.take(embed_table, jnp.clip(local_row, 0, vocab_rows - 1), axis=0)
    summed = lax.psum_scatter(
        jnp.where(inside[:, None], picked.astype(jnp.float32), 0.0).astype(jnp.bfloat16),
        ("ctx", "role"),
        scatter_dimension=0,
        tiled=True,
    )
    partial_latent = jnp.dot(summed, latent_down, preferred_element_type=jnp.float32)
    latent = lax.psum(partial_latent, "tp")
    row_index = group_index * block_rows + jnp.arange(block_rows, dtype=jnp.int32)
    prompt_keys_here = finish_keys(latent, latent_gain, row_index // prompt_count)
    step_rows = decode_query.shape[0] * STEPS
    own_latent = lax.dynamic_slice_in_dim(latent, tp_index * step_rows, step_rows, 0)
    decode_pos = (cache_length[:, None] + jnp.arange(STEPS, dtype=jnp.int32)[None, :]).reshape(-1)
    fresh_keys = finish_keys(own_latent, latent_gain, decode_pos)
    arrived = passed_along(prompt_keys_here, "role", 1)
    prompt_keys = lax.all_gather(arrived, "ctx", axis=0, tiled=True)
    heads_here = prefill_query.shape[1]
    start_state = (
        jnp.full((heads_here, block_rows), masked_fill, jnp.float32),
        jnp.zeros((heads_here, block_rows), jnp.float32),
        jnp.zeros((heads_here, block_rows, LAT), jnp.float32),
    )
    block_keys = lax.all_gather(prompt_keys_here, "ctx", axis=0, tiled=True)

    def attend(state):
        key_rows = jnp.arange(block_keys.shape[0], dtype=jnp.int32)
        allowed = (key_rows[None, :] % prompt_count == row_index[:, None] % prompt_count) & (
            key_rows[None, :] <= row_index[:, None]
        )
        scores = (
            jnp.einsum("qhc,kc->hqk", prefill_query, block_keys, preferred_element_type=jnp.float32)
            * score_scale
        )

        def weigh_values(weights):
            return jnp.einsum(
                "hqk,kc->hqc", weights, block_keys[:, :LAT], preferred_element_type=jnp.float32
            )

        return merge_parts(state, partial_part(scores, allowed[None], weigh_values))

    def unchanged(state):
        return state

    folded = lax.cond(section == 0, attend, unchanged, start_state)
    prefill_out = (
        jnp.transpose(folded[2] / folded[1][..., None], (1, 0, 2))
        .astype(jnp.bfloat16)
        .reshape(block_rows, heads_here * LAT)
    )
    all_heads = decode_query.shape[2]

    def decode_rows(unused):
        row_count = decode_query.shape[0]
        fresh = fresh_keys.reshape(row_count, STEPS, -1)
        cache_scores = (
            jnp.einsum(
                "rshc,rkc->rshk", decode_query, latent_cache, preferred_element_type=jnp.float32
            )
            * score_scale
        )
        cache_ok = (
            jnp.arange(latent_cache.shape[1], dtype=jnp.int32)[None, :] < cache_length[:, None]
        )[:, None, None, :]

        def weigh_cache(weights):
            return jnp.einsum(
                "rshk,rkc->rshc",
                weights,
                latent_cache[..., :LAT],
                preferred_element_type=jnp.float32,
            )

        state = partial_part(cache_scores, cache_ok, weigh_cache)
        fresh_scores = (
            jnp.einsum("rshc,rtc->rsht", decode_query, fresh, preferred_element_type=jnp.float32)
            * score_scale
        )
        step_index = jnp.arange(STEPS, dtype=jnp.int32)
        fresh_ok = (step_index[None, :] <= step_index[:, None])[None, :, None, :]

        def weigh_fresh(weights):
            return jnp.einsum(
                "rsht,rtc->rshc", weights, fresh[..., :LAT], preferred_element_type=jnp.float32
            )

        state = merge_parts(state, partial_part(fresh_scores, fresh_ok, weigh_fresh))
        for prompt in range(prompt_count):
            prompt_block = prompt_keys[prompt::prompt_count]

            def add_prompt(current, block_keys=prompt_block):
                scores = (
                    jnp.einsum(
                        "rshc,kc->rshk",
                        decode_query,
                        block_keys,
                        preferred_element_type=jnp.float32,
                    )
                    * score_scale
                )

                def weigh_prompt(weights):
                    return jnp.einsum(
                        "rshk,kc->rshc",
                        weights,
                        block_keys[:, :LAT],
                        preferred_element_type=jnp.float32,
                    )

                return merge_parts(
                    current, partial_part(scores, jnp.ones((1, 1, 1, 1), jnp.bool_), weigh_prompt)
                )

            def keep_state(current):
                return current

            state = lax.cond(prompt_owner[prompt] == group_index, add_prompt, keep_state, state)
        return (
            (state[2] / state[1][..., None])
            .astype(jnp.bfloat16)
            .reshape(row_count * STEPS, all_heads, LAT)
        )

    def empty_rows(unused):
        return jnp.zeros((step_rows, all_heads, LAT), jnp.bfloat16)

    decode_result = lax.cond(section == 1, decode_rows, empty_rows, jnp.int32(0))
    decode_out = lax.all_to_all(
        decode_result, "tp", split_axis=1, concat_axis=0, tiled=True
    ).reshape(block_rows, heads_here * LAT)
    return jnp.where(section == 0, prefill_out, decode_out)[None]


def solution(mesh):
    in_specs = (
        P("role", "ctx"),
        P(("ctx", "role"), "tp"),
        P("tp", None),
        P(),
        P("ctx", "tp", None),
        P(("ctx", "tp"), None, None, None),
        P(("ctx", "tp"), None, None),
        P(("ctx", "tp")),
        P(),
    )
    out_specs = P("role", "ctx", "tp")
    return jax.shard_map(shards, mesh=mesh, in_specs=in_specs, out_specs=out_specs, check_vma=False)
```

profile of v0, /device:TPU:88, one launch (start us, length us, event | category | flops | bytes accessed | tf_op | source)
XLA Modules:
  0.0 551.2 jit_solution(13469879500511097529)
XLA Ops:
  6.5 71.2 %all-gather = s32[32,1,128]{2,1,0:T(1,128)S(1)} all-gather(s32[1,1,128]{2,1,0:T(1,128)} %bitcast.145), channel_id=1, replica_groups=mesh['ctx'=16,'tp'=8,'role'=2] {'ctx','role'}, dimensions={0}, use_global_device_ids=true | all-gather | bytes 16896 | tf_op jit(solution)/shard_map/all_gather | solution.py:80
  77.8 22.3 %gather_fusion = bf16[4096,896]{1,0:T(8,128)(2,1)} fusion(bf16[2048,896]{1,0:T(8,128)(2,1)} %param.18, s32[4096]{0:T(1024)S(1)} %broadcast_clamp_fusion), kind=kCustom, calls=%fused_computation | custom fusion | bytes 14696448 | tf_op jit(solution)/shard_map/jit(_take)/gather | solution.py:83
  100.1 7.2 %select_convert_fusion = bf16[4096,896]{1,0:T(8,128)(2,1)} fusion(bf16[4096,896]{1,0:T(8,128)(2,1)} %gather_fusion, pred[4096]{0:T(1024)(128)(4,1)S(1)} %get-tuple-element.155, pred[4096]{0:T(1024)(128)(4,1)S(1)} %and_bitcast_fusion), kind=kLoop, calls=%fused_computation.98 | loop fusion | flops 14680064 | bytes 14688256 | tf_op jit(solution)/shard_map/convert_element_type | solution.py:85
  107.5 177.6 %reduce-scatter.2.cloned.1.call-done = bf16[128,896]{1,0:T(8,128)(2,1)} async-done(((bf16[4096,896]{1,0:T(8,128)(2,1)}), bf16[128,896]{1,0:T(8,128)(2,1)}) %reduce-scatter.2.cloned.1.call-update) | async-done | bytes 229392 | tf_op jit(solution)/shard_map/reduce_scatter | solution.py:84
  285.1 2.1 fusion.91
  287.3 67.2 %all-reduce.2.cloned.1.call-done = f32[128,576]{1,0:T(8,128)} async-done(((f32[128,576]{1,0:T(8,128)}), f32[128,576]{1,0:T(8,128)}) %all-reduce.2.cloned.1.call-update) | async-done | bytes 294928 | tf_op jit(solution)/shard_map/psum | solution.py:91
  354.5 1.1 multiply_reduce_fusion.2
  355.6 1.0 multiply_convert_fusion
  356.7 1.2 fusion.75
  358.0 1.3 collective-permute-start
  359.3 7.4 %collective-permute-done = bf16[128,576]{1,0:T(8,128)(2,1)S(1)} collective-permute-done((bf16[128,576]{1,0:T(8,128)(2,1)S(1)}, bf16[128,576]{1,0:T(8,128)(2,1)S(1)}, u32[]{:S(2)}, u32[]{:S(2)}) %collective-permute-start) | collective-permute-done | bytes 147488 | tf_op jit(solution)/shard_map/ppermute | solution.py:19
  369.0 0.9 fusion.83
  370.9 67.1 %all-gather.6.cloned.1.call-done = bf16[2048,576]{1,0:T(8,128)(2,1)} async-done(((bf16[128,576]{1,0:T(8,128)(2,1)}), bf16[2048,576]{1,0:T(8,128)(2,1)}) %all-gather.6.cloned.1.call-update) | async-done | bytes 2359312 | tf_op jit(solution)/shard_map/all_gather | solution.py:99
  437.9 79.3 %conditional.5 = (bf16[16,64,512]{2,1,0:T(8,128)(2,1)S(1)}) conditional(s32[]{:T(128)} %convert_element_type.67, () %tuple.35, (s32[2]{0:T(128)S(1)}, s32[]{:T(128)}, s32[8]{0:T(128)S(1)}, bf16[8,2,64,576]{3,2,1,0:T(8,128)(2,1)}, bf16[8,512,576]{1,2,0:T(8,128)(2,1)}, /*index=5*/bf16[16,576]{1,0:T(8,128)(2,1)S(1)}, bf16[2048,576]{1,0:T(8,128)(2,1)}) %tuple.95), branch_computations={%region_8.9_spmd, %region_9.22_spmd} | conditional | flops 5738102784 | bytes 96066376 | solution.py:210
  438.0 3.9 fusion.52
  442.6 2.1 fusion.90
  444.8 7.7 %copy.58 = bf16[8,512,576]{2,1,0:T(8,128)(2,1)} copy(bf16[8,512,576]{1,2,0:T(8,128)(2,1)} %get-tuple-element.139) | data formatting | bytes 9437184 | tf_op jit(solution)/shard_map
  452.5 4.4 fusion.51
  457.0 3.6 multiply_add_fusion.6
  460.5 2.9 copy.59
  464.7 49.9 %conditional = ((f32[8,2,64]{2,1,0:T(2,128)S(1)}, f32[8,2,64]{2,1,0:T(2,128)S(1)}, f32[8,2,64,512]{3,2,1,0:T(8,128)})) conditional(s32[]{:T(128)} %convert_element_type.48, (f32[8,2,64]{2,1,0:T(2,128)S(1)}, f32[8,2,64]{2,1,0:T(2,128)S(1)}, f32[8,2,64,512]{3,2,1,0:T(8,128)}) %tuple.91, (bf16[2048,576]{0,1:T(8,128)(2,1)S(1)}, ...), branch_computations={%region_14.14_spmd, %region_15.17_spmd} | conditional | flops 2291666944 | bytes 27332668 | solution.py:200
  464.9 41.0 %slice.39 = bf16[1024,576]{0,1:T(8,128)(2,1)} slice(bf16[2048,576]{0,1:T(8,128)(2,1)S(1)} %get-tuple-element.70), slice={[0:2048:2], [0:576:1]} | slice | bytes 2359296 | tf_op jit(solution)/shard_map/cond/branch_1_fun/slice | solution.py:172
  505.9 3.6 multiply_reduce_fusion
  509.5 0.9 fusion.26
  510.7 3.9 multiply_add_fusion.2
  515.2 1.8 divide_convert_fusion
  517.2 1.5 copy.60
  518.8 4.2 all-to-all-start
  524.7 14.4 %all-to-all-done = bf16[16,64,512]{2,0,1:T(8,128)(2,1)} async-done(((bf16[16,64,512]{2,0,1:T(8,128)(2,1)}), bf16[16,64,512]{2,0,1:T(8,128)(2,1)}, u32[]{:S(2)}, u32[]{:S(2)}) %all-to-all-start) | async-done | bytes 1048608 | tf_op jit(solution)/shard_map/all_to_all | solution.py:211
  539.1 2.8 copy.61
  541.9 1.6 reshape.268
  543.5 1.1 broadcast_select_fusion
  (56 shorter events, 7.2 us)
Async XLA Ops:
  6.5 278.6 %copy-start = (bf16[896,576]{0,1:T(8,128)(2,1)S(1)}, bf16[896,576]{0,1:T(8,128)(2,1)}, u32[]{:S(2)}) copy-start(bf16[896,576]{0,1:T(8,128)(2,1)} %param.19) | copy-start | bytes 3096580
  6.5 278.6 %reduce-scatter.2.cloned.1.call-start = ((), (), s32[]{:S(2)}) async-start(), calls=%async_computation.2 | async-start | bytes 7569408 | tf_op jit(solution)/shard_map/reduce_scatter | solution.py:84
  107.4 248.2 %copy-start.6 = (f32[512]{0:T(512)S(1)}, f32[512]{0:T(512)}, u32[]{:S(2)}) copy-start(f32[512]{0:T(512)} %param.20) | copy-start | bytes 6148
  107.4 260.6 %copy-start.7 = (s32[8]{0:T(128)S(1)}, s32[8]{0:T(128)}, u32[]{:S(2)}) copy-start(s32[8]{0:T(128)} %param.24) | copy-start | bytes 100
  107.4 330.5 %copy-start.8 = (s32[2]{0:T(128)S(1)}, s32[2]{0:T(128)}, u32[]{:S(2)}) copy-start(s32[2]{0:T(128)} %param.25) | copy-start | bytes 28
  107.4 247.1 %all-reduce.2.cloned.1.call-start = ((), (), s32[]{:S(2)}) async-start(), calls=%async_computation.3 | async-start | bytes 655360 | tf_op jit(solution)/shard_map/psum | solution.py:91
  287.3 150.7 %all-gather.6.cloned.1.call-start = ((), (), s32[]{:S(2)}) async-start(), calls=%async_computation.5 | async-start | bytes 2785280 | tf_op jit(solution)/shard_map/all_gather | solution.py:99
  358.0 9.5 %copy-start.4 = (bf16[128,576]{1,0:T(8,128)(2,1)}, bf16[128,576]{1,0:T(8,128)(2,1)S(1)}, u32[]{:S(2)}) copy-start(bf16[128,576]{1,0:T(8,128)(2,1)S(1)} %pad_maximum_fusion) | copy-start | bytes 442372
  358.0 8.7 %collective-permute-start = (bf16[128,576]{1,0:T(8,128)(2,1)S(1)}, bf16[128,576]{1,0:T(8,128)(2,1)S(1)}, u32[]{:S(2)}, u32[]{:S(2)}) collective-permute-start(bf16[128,576]{1,0:T(8,128)(2,1)S(1)} %pad_maximum_fusion), channel_id=1, source_target_pairs={{0,1},{2,3},{4,5},{6,7},{8,9},{10,11},{12,13},{14,15},{16,17},{18,... | collective-permute-start | bytes 442376 | tf_op jit(solution)/shard_map/ppermute | solution.py:19
  366.7 0.7 copy-start.5
  367.4 155.7 %all-gather.4.cloned.1.call-start = ((), (), s32[]{:S(2)}) async-start(), calls=%async_computation.4 | async-start | bytes 2785280 | tf_op jit(solution)/shard_map/all_gather | solution.py:106
  509.5 1.3 copy-start.2
  518.8 20.3 %all-to-all-start = ((bf16[16,64,512]{2,0,1:T(8,128)(2,1)}), bf16[16,64,512]{2,0,1:T(8,128)(2,1)}, u32[]{:S(2)}, u32[]{:S(2)}) async-start(bf16[16,64,512]{2,0,1:T(8,128)(2,1)} %copy.60), calls=%async_computation.1 | async-start | bytes 2097152 | tf_op jit(solution)/shard_map/all_to_all | solution.py:211
  541.9 2.7 copy-start.1
Sparse Core Ops, SparseCore 0:
  107.5 177.5 reduce-scatter.1
  287.4 67.0 all-reduce.1
  367.5 70.3 all-gather.5
  439.7 70.6 all-gather.3
where the time goes:
time: 552 us; the launch traced here: 551 us
  waiting for transfers between devices  334 us (61%)
  local copies, waits for them, and re-layouts  83 us (15%)
  blocking collectives  71.2 us (13%)
  matrix products  23.5 us (4%)
  other arithmetic  18.5 us (3%)
  between operations  13.3 us (2%)
  starting transfers between devices  5.67 us (1%)
    reduce_scatter x1, waiting for transfers between devices, shards(): lax.psum_scatter(jnp.where(inside[:, None], picked.astype(jnp.float32), 0...  178 us
    all_gather x1, blocking collectives, shards(): every_id = lax.all_gather(token_ids, ('ctx', 'role'), axis=0, tiled=True)  71.2 us
    psum x1, waiting for transfers between devices, shards(): latent = lax.psum(partial_latent, 'tp')  67.2 us
    all_gather x1, waiting for transfers between devices, shards(): prompt_keys = lax.all_gather(arrived, 'ctx', axis=0, tiled=True)  67.1 us
    slice x1, local copies, waits for them, and re-layouts, decode_rows(): prompt_block = prompt_keys[prompt::prompt_count]  41 us
    gather x1, local copies, waits for them, and re-layouts, shards(): jnp.take(embed_table, jnp.clip(local_row, 0, vocab_rows - 1), axis=0)  22.3 us
    all_to_all x1, waiting for transfers between devices, shards(): lax.all_to_all(decode_result, 'tp', split_axis=1, concat_axis=0, tiled=True)  14.4 us
  transfers between devices with their start and end apart: 6, of which 5 were waited for; matrix products, arithmetic and copies ran while one was open for 15% of the time, Pallas kernels for 0%

commit v1 on v0

v1 whole, which is shorter than its diff:
```python
import jax
import jax.numpy as jnp
import numpy as np
from jax import lax
from jax.experimental import pallas as pl
from jax.experimental.pallas import tpu as pltpu
from jax.sharding import Mesh
from jax.sharding import PartitionSpec as P

LAT = 512
KVW = 576
STEPS = 2
WIDE = 640
SLOTS = 16
KEPT = 48
SIDE = 16 * KEPT
KEYS = 2048

score_scale = 0.07216878364870322
masked_fill = -1e30
norm_eps = 1e-06
rope_base = 10000.0
bf16 = jnp.bfloat16
f32 = jnp.float32
SMEM = pltpu.SMEM
VMEM = pltpu.VMEM

HOLDERS = ("ylo", "z", "role")
PLANE = ("ylo", "role", "x")
TP = ("x", "core")


def iota(shape, axis):
    return lax.broadcasted_iota(jnp.int32, shape, axis)


def ones_where(flags):
    return jnp.where(flags, 1.0, 0.0).astype(bf16)


def dot(left, right):
    return lax.dot_general(left, right, (((1,), (0,)), ((), ())), preferred_element_type=f32)


def dot_nt(left, right):
    return lax.dot_general(left, right, (((1,), (1,)), ((), ())), preferred_element_type=f32)


def whole_loop(count, body, unroll=1):
    def step(index, carry):
        body(index)
        return carry

    lax.fori_loop(0, count, step, 0, unroll=unroll)


def aligned(index, size):
    return pl.ds(pl.multiple_of(index * size, size), size)


def select_kernel(place, ids, table, down, partial, hots, lows, chosen, table_here, down_here, sems):
    holder = place[0]
    table_copy = pltpu.make_async_copy(table, table_here, sems.at[0])
    down_copy = pltpu.make_async_copy(down, down_here, sems.at[1])
    table_copy.start()
    down_copy.start()

    def mark(block):
        tokens = ids[pl.ds(block, 1), :]
        span = aligned(block, 128)
        hots[:, span] = ones_where(iota((16, 128), 0) == (tokens >> 7) - holder * 16)
        lows[:, span] = ones_where(iota((128, 128), 0) == (tokens & 127))

    whole_loop(32, mark, 8)
    odd = ((iota((16, 4096), 1) >> 7) & 1) == 1
    both = hots[...]
    decodes = jnp.where(odd, both, jnp.zeros_like(both))
    in_prompt = dot_nt(both - decodes, lows[...]) > 0.5
    alone = (dot_nt(decodes, lows[...]) > 0.5) & jnp.logical_not(in_prompt)
    upper = ones_where(iota((128, 128), 0) < iota((128, 128), 1))
    all_ones = jnp.ones((128, 128), bf16)
    row = iota((8 * SLOTS, 128), 0)
    wanted = ((row & 15) * 8 + (((row >> 4) - holder) & 7)).astype(f32)
    before = jnp.zeros((1, 128), f32)
    ranks = []
    for present in (in_prompt, alone):
        flags = ones_where(present)
        within = dot(flags, upper)
        totals = dot(flags, all_ones)
        lines = []
        for step in range(16):
            lines.append(within[step : step + 1, :] + before)
            before = before + totals[step : step + 1, :]
        ranks.append(lines)
    for step in range(16):
        rank = jnp.where(alone[step : step + 1, :], ranks[1][step], -1.0)
        rank = jnp.where(in_prompt[step : step + 1, :], ranks[0][step], rank)
        chosen[:, step * 128 : (step + 1) * 128] = ones_where(wanted == rank)
    table_copy.wait()
    rows = dot(chosen[...], table_here[...]).astype(bf16)
    down_copy.wait()
    partial[...] = dot_nt(rows, down_here[...]).reshape(partial.shape)


def place_kernel(place, ids, columns, kept, fits, highs, lows, quads, holders, sheet, sheet_b):
    ylo, zed, ex, core, section = place[0], place[1], place[2], place[3], place[4]
    square = (128, 128)
    lane = iota((8, 128), 1)
    target = iota(square, 1)
    mover = ones_where(iota(square, 0) == jnp.where(target < 64, 2 * target, 2 * target - 127))
    plain = ids[pl.ds(0, 16, stride=2), :]
    coarse = (plain >> 8).astype(f32).astype(bf16)
    fine = (plain & 255).astype(f32).astype(bf16)
    moved = dot(coarse, mover) * 256.0 + dot(fine, mover)
    sheet[0:16, :] = moved.astype(jnp.int32)
    even = sheet[pl.ds(0, 8, stride=2), :]
    odd = sheet[pl.ds(1, 8, stride=2), :]
    first = jnp.where(lane < 64, even, pltpu.roll(odd, 64, 1))
    second = jnp.where(lane < 64, pltpu.roll(even, 64, 1), odd)
    tokens = jnp.concatenate([first, second, ids[pl.ds(1, 16, stride=2), :]], axis=0)
    sheet[0:32, :] = tokens

    def mark(block):
        line = sheet[pl.ds(block, 1), :]
        span = aligned(block, 128)
        highs[:, span] = ones_where(iota((512, 128), 0) == (line >> 7))
        lows[:, span] = ones_where(iota(square, 0) == (line & 127))

    whole_loop(32, mark, 8)
    in_prompt = dot_nt(lows[:, :KEYS], highs[:, :KEYS]) > 0.5
    alone = (dot_nt(lows[:, KEYS:], highs[:, KEYS:]) > 0.5) & jnp.logical_not(in_prompt)
    below = ones_where(iota(square, 1) < iota(square, 0))
    all_ones = jnp.ones(square, bf16)
    wide = (512, 512)
    same = (iota(wide, 0) // 16) == (iota(wide, 1) // 16)
    in_holder = ones_where(same & (iota(wide, 0) < iota(wide, 1)))
    prompt_flags = ones_where(in_prompt)
    alone_flags = ones_where(alone)
    prompt_columns = dot(all_ones, prompt_flags).astype(bf16)
    alone_columns = dot(all_ones, alone_flags).astype(bf16)
    prompt_rank = dot(below, prompt_flags) + dot(prompt_columns, in_holder)
    alone_rank = (
        dot(below, alone_flags) + dot(alone_columns, in_holder) + dot(prompt_columns, ones_where(same))
    )
    rank = jnp.where(in_prompt, prompt_rank, jnp.where(alone, alone_rank, 0.0))
    top_rank = jnp.max(jnp.max(rank, axis=0, keepdims=True), axis=1, keepdims=True)
    coded = (jnp.minimum(rank, 127.0) + jnp.where(in_prompt, 128.0, 0.0)).astype(bf16)
    pieces = []
    for chunk in range(4):
        span = slice(chunk * 1024, (chunk + 1) * 1024)
        looked = dot(coded, highs[:, span]) * lows[:, span].astype(f32)
        line = jnp.sum(looked, axis=0, keepdims=True)
        for part in range(8):
            pieces.append(line[:, part * 128 : (part + 1) * 128])
    value = jnp.concatenate(pieces, axis=0).astype(jnp.int32)
    ranks = value & 127
    holder = tokens >> 11
    tp_of = (ranks + holder) & 7
    quad = tp_of * 16 + (ranks >> 3)
    sheet[0:32, :] = quad
    sheet[32:64, :] = holder
    sheet[64:96, :] = jnp.where(value >= 128, -1, tp_of)

    def spot(block, source):
        span = aligned(block, 128)
        quads[:, span] = ones_where(iota(square, 0) == sheet[pl.ds(source, 1), :])
        holders[:, span] = ones_where(iota(square, 0) == sheet[pl.ds(source + 32, 1), :])

    whole_loop(16, lambda block: spot(block, block), 8)
    for part in range(2):
        spot(16 + part, 16 + part * 8 + zed)
    spot(18, 16 + ylo * 8 + zed)
    counted = dot_nt(quads[:, :KEYS], holders[:, :KEYS])
    newest = dot_nt(quads[:, KEYS : KEYS + 256], holders[:, KEYS : KEYS + 256])
    held = (counted + newest) > 0.5
    held_flags = ones_where(held)
    up, down = iota(square, 0), iota(square, 1)
    same_tp = (up // 16) == (down // 16)
    same_pool = ((up >> 4) == (down >> 4)) & ((up & 1) == (down & 1))
    pool = ones_where(same_pool)
    before = ones_where(same_pool & (up < down))
    in_tp = ones_where(same_tp & (down < up))
    position = dot(in_tp, held_flags) + dot(dot(ones_where(same_tp), held_flags).astype(bf16), before)
    position = jnp.where(held, jnp.minimum(position, 255.0), 255.0)
    gather_tp = ones_where(up == (down >> 4))
    sheet_b[...] = dot(dot(gather_tp, ones_where(counted > 0.5)).astype(bf16), pool)

    def extras(plane, worst):
        fresh = []
        owners = []
        for part in range(2):
            source = 16 + part * 8 + plane
            fresh.append(ones_where(iota(square, 0) == sheet[pl.ds(source + 64, 1), :]))
            owners.append(ones_where(iota(square, 0) == sheet[pl.ds(source + 32, 1), :]))
        added = dot_nt(jnp.concatenate(fresh, axis=1), jnp.concatenate(owners, axis=1))
        needed = sheet_b[...] + dot(added.astype(bf16), pool)
        return jnp.maximum(worst, needed)

    needed = lax.fori_loop(0, 8, extras, jnp.zeros(square, f32), unroll=4)
    needed = jnp.max(jnp.max(needed, axis=0, keepdims=True), axis=1, keepdims=True)
    enough = (top_rank < 8.0 * SLOTS) & (needed <= float(KEPT))
    fits[0, 0] = jnp.max(jnp.where(enough, 1, 0))
    position_b = position.astype(bf16)
    looked = dot(position_b, holders[...]) * quads[...].astype(f32)
    line = jnp.sum(looked, axis=0, keepdims=True)
    found = [line[:, block * 128 : (block + 1) * 128] for block in range(19)]
    found = jnp.concatenate(found + [jnp.zeros((5, 128), f32)], axis=0)
    own = 16 + ylo * 8 + zed
    quad_rows = jnp.concatenate(
        [sheet[0:16, :], jnp.zeros((2, 128), jnp.int32), sheet[pl.ds(own, 1), :], jnp.zeros((5, 128), jnp.int32)], axis=0
    )
    holder_rows = jnp.concatenate(
        [sheet[32:48, :], jnp.zeros((2, 128), jnp.int32), sheet[pl.ds(own + 32, 1), :], jnp.zeros((5, 128), jnp.int32)],
        axis=0,
    )
    tp_rows = quad_rows >> 4
    source = ((holder_rows >> 4) * 2 + (holder_rows & 1)) * 4 + (tp_rows >> 1)
    side = jnp.where((tp_rows & 1) == core, 0, SIDE)
    final = found + (source * KEPT + side).astype(f32)
    tp_index = ex * 2 + core
    turned = pltpu.roll(final, (128 - tp_index * 16) % 128, 1)
    turned = jnp.where(iota((24, 128), 1) < 16, turned, -1.0)
    final = jnp.where(iota((24, 128), 0) == 18, turned, final)
    final = jnp.concatenate([final, jnp.zeros((104, 128), f32)], axis=0)
    columns[...] = jnp.transpose(final).astype(jnp.int32)
    sheet_b[...] = position
    mine = sheet_b[pl.ds(pl.multiple_of(tp_index * 16, 16), 16), :].astype(bf16)
    spread = dot(mine, ones_where(up == (ylo * 8 + (down >> 4)) * 2 + section))
    few = (16, 128)
    spread = jnp.where((iota(few, 1) & 15) == iota(few, 0), spread, 0.0)
    kept[...] = jnp.broadcast_to(jnp.sum(spread, axis=0, keepdims=True), kept.shape)


def finish_kernel(parts, gain, sent):
    latent = parts[0]
    for tp in range(1, parts.shape[0]):
        latent = latent + parts[tp]
    plain = latent[:, :LAT]
    scaled = plain * lax.rsqrt(jnp.mean(plain * plain, axis=-1, keepdims=True) + norm_eps) * gain[...]
    rotary = latent[:, LAT:]
    coarse = rotary.astype(bf16)
    fine = (rotary - coarse.astype(f32)).astype(bf16)
    row = jnp.concatenate([scaled.astype(bf16), coarse, fine], axis=-1)
    for peer in range(sent.shape[0]):
        sent[peer] = row


def keep_kernel(kept, rows, sent):
    chosen = iota((KEPT, 128), 0).astype(f32) == kept[0:1, :]
    row = dot(ones_where(chosen), rows[...]).astype(bf16)
    for peer in range(sent.shape[0]):
        sent[peer] = row


def cache_kernel(lengths, query, cache, out, level):
    length = lengths[pl.program_id(0)]
    scores = dot(query[0], cache[0]) * score_scale
    scores = jnp.where(iota(scores.shape, 1) < length, scores, masked_fill)
    highest = jnp.max(scores, axis=-1, keepdims=True)
    weights = jnp.exp(scores - highest)
    total = jnp.sum(weights, axis=-1, keepdims=True)
    out[...] = (dot_nt(weights.astype(bf16), cache[0, :LAT, :]) / total).astype(bf16)
    level[...] = jnp.broadcast_to(highest + jnp.log(total), level.shape)


def hot_rows(hot, columns, prompt, side):
    for block in range(8):
        wanted = jnp.sum(jnp.where(iota((128, 128), 1) == prompt * 8 + block, columns[...], 0), axis=1, keepdims=True)
        hot[block * 128 : (block + 1) * 128, :] = ones_where(iota((128, SIDE), 1) == wanted - side * SIDE)


def fresh_hot(columns, side):
    return ones_where(iota((128, SIDE), 1) == columns[:, 18:19] - side * SIDE)


def put_keys(keys, span, found, factor):
    turning = found[:, LAT:]
    turning = turning + pltpu.roll(turning, 64, 1)
    turned = turning * factor + pltpu.roll(turning, 32, 1) * pltpu.roll(factor, 64, 1)
    keys[span, :LAT] = found[:, :LAT].astype(bf16)
    keys[span, LAT:] = turned[:, : KVW - LAT].astype(bf16)


def copy_in(source, target, sem):
    copy = pltpu.make_async_copy(source, target, sem)
    copy.start()
    copy.wait()


def fold(query, some, allowed, highest, total, mixed, span):
    scores = dot_nt(query, some[:, :]) * score_scale
    if allowed is not None:
        scores = jnp.where(allowed(scores.shape), scores, masked_fill)
    old = highest[span, 0:1]
    new = jnp.maximum(old, jnp.max(scores, axis=-1, keepdims=True))
    weights = jnp.exp(scores - new)
    factor = jnp.exp(old - new)
    summed = total[span, 0:1] * factor + jnp.sum(weights, axis=-1, keepdims=True)
    mixed[span, :] = mixed[span, :] * factor + dot(weights.astype(bf16), some[:, :LAT])
    highest[span, :] = jnp.broadcast_to(new, (scores.shape[0], 128))
    total[span, :] = jnp.broadcast_to(summed, (scores.shape[0], 128))


def near_kernel(place, owner, slots, columns, near, hot):
    group = place[0] * 8 + place[1]

    @pl.when(place[4] == 1)
    def _():
        near[KEYS : KEYS + 128, :] = dot(fresh_hot(columns, 0), slots[...]).astype(bf16)

        def open_prompt(prompt):
            @pl.when(owner[prompt] == group)
            def _():
                hot_rows(hot, columns, prompt, 0)

                def open_part(part):
                    near[aligned(prompt * 2 + part, 512), :] = dot(hot[aligned(part, 512), :], slots[...]).astype(bf16)

                whole_loop(2, open_part)

        whole_loop(2, open_prompt)


def decode_kernel(
    place, owner, fits, near, others, columns, factors, new_factors, query, earlier, level, spare, spare_new,
    out, keys, hot, highest, total, mixed, lines, sem
):
    group = place[0] * 8 + place[1]
    fitting = fits[0, 0] == 1

    @pl.when(place[4] == 1)
    def _():
        @pl.when(fitting)
        def _():
            found = near[KEYS : KEYS + 128, :].astype(f32) + dot(fresh_hot(columns, 1), others[...])
            put_keys(keys, slice(KEYS, KEYS + 128), found, new_factors[...])

        @pl.when(jnp.logical_not(fitting))
        def _():
            copy_in(spare_new, keys.at[pl.ds(KEYS, 128)], sem)

        newest = keys[KEYS : KEYS + 128, :]

        def begin(piece):
            span = aligned(piece, 512)
            scores = dot_nt(query[span, :], newest) * score_scale
            key = iota(scores.shape, 1)
            row = iota(scores.shape, 0) + piece * 512
            allowed = ((key >> 1) == (row >> 7)) & ((key & 1) <= ((row >> 6) & 1))
            scores = jnp.where(allowed, scores, masked_fill)
            old = level[span, 0:1]
            new = jnp.maximum(old, jnp.max(scores, axis=-1, keepdims=True))
            weights = jnp.exp(scores - new)
            factor = jnp.exp(old - new)
            summed = factor + jnp.sum(weights, axis=-1, keepdims=True)
            mixed[span, :] = earlier[span, :].astype(f32) * factor + dot(weights.astype(bf16), newest[:, :LAT])
            highest[span, :] = jnp.broadcast_to(new, (512, 128))
            total[span, :] = jnp.broadcast_to(summed, (512, 128))

        whole_loop(2, begin)

        def add_prompt(prompt):
            @pl.when(owner[prompt] == group)
            def _():
                @pl.when(fitting)
                def _():
                    hot_rows(hot, columns, prompt, 1)

                    def open_part(part):
                        span = aligned(prompt * 2 + part, 512)
                        found = near[span, :].astype(f32) + dot(hot[aligned(part, 512), :], others[...])
                        put_keys(keys, span, found, factors[aligned(part, 512), :])

                    whole_loop(2, open_part)

                @pl.when(jnp.logical_not(fitting))
                def _():
                    copy_in(spare.at[pl.ds(prompt * 1024, 1024)], keys.at[pl.ds(prompt * 1024, 1024)], sem)

                def add_part(piece):
                    span = aligned(piece, 512)
                    fold(query[span, :], keys[aligned(prompt, 1024), :], None, highest, total, mixed, span)

                whole_loop(2, add_part)

        whole_loop(2, add_prompt)

        for piece in range(4):
            span = slice(piece * 256, (piece + 1) * 256)
            quotient = mixed[span, :] / total[span, 0:1]
            for column in range(4):
                lines[column, span, :] = quotient[:, column * 128 : (column + 1) * 128]

        def tp_rows(tp):
            for head in range(8):
                for column in range(4):
                    some = lines[column, pl.ds(tp * 8 + head, 16, stride=64), :]
                    start = head * LAT + column * 128
                    out[aligned(tp, 16), start : start + 128] = some.astype(bf16)

        whole_loop(8, tp_rows)


def prefill_kernel(
    place, fits, slots, others, columns, factors, query, spare, out, keys, hot, highest, total, mixed, lines, sem
):
    group = place[0] * 8 + place[1]
    fitting = fits[0, 0] == 1

    @pl.when(place[4] == 0)
    def _():
        highest[...] = jnp.full(highest.shape, masked_fill, f32)
        total[...] = jnp.zeros(total.shape, f32)
        mixed[...] = jnp.zeros(mixed.shape, f32)

        def add_prompt(prompt):
            @pl.when(fitting)
            def _():
                for side in range(2):
                    hot_rows(hot, columns, prompt, side)

                    def open_part(part, side=side):
                        span = aligned(part, 512)
                        if side == 0:
                            lines[span, :] = dot(hot[span, :], slots[...])
                        else:
                            found = lines[span, :] + dot(hot[span, :], others[...])
                            put_keys(keys, span, found, factors[span, :])

                    whole_loop(2, open_part)

            @pl.when(jnp.logical_not(fitting))
            def _():
                copy_in(spare.at[pl.ds(prompt * 1024, 1024)], keys, sem)

            def causal(shape):
                last = (iota((shape[0], 1), 0) & 63) + group * 64
                return iota(shape, 1) <= last

            span = aligned(prompt, 512)
            fold(query[span, :], keys[...], causal, highest, total, mixed, span)
            mixed[span, :] = mixed[span, :] / total[span, 0:1]

        whole_loop(2, add_prompt)

        def head_rows(head):
            for column in range(4):
                for prompt in range(2):
                    some = mixed[pl.ds(pl.multiple_of(prompt * 512 + head * 64, 64), 64), column * 128 : (column + 1) * 128]
                    highest[pl.ds(prompt, 64, stride=2), :] = some
                out[:, pl.ds(pl.multiple_of(head * LAT + column * 128, 128), 128)] = highest[0:128, :].astype(bf16)

        whole_loop(8, head_rows)


def rope_factors(position):
    frequency = np.float32(rope_base) ** (-np.arange(32, dtype=np.float32) / np.float32(32))
    angles = position[:, None] * frequency[None, :]
    if isinstance(position, np.ndarray):
        angles = angles.astype(np.float32).astype(np.float64)
        cosine, sine = np.cos(angles), np.sin(angles)
        return np.concatenate([cosine, cosine, -sine, sine], axis=-1).astype(np.float32)
    cosine, sine = jnp.cos(angles), jnp.sin(angles)
    return jnp.concatenate([cosine, cosine, -sine, sine], axis=-1)


def finish_keys(latent, latent_gain, position):
    plain = latent[:, :LAT]
    scaled = plain * lax.rsqrt(jnp.mean(plain * plain, axis=-1, keepdims=True) + norm_eps) * latent_gain
    factors = rope_factors(position.astype(f32))
    rotary = latent[:, LAT:]
    swapped = jnp.concatenate([rotary[:, 32:], rotary[:, :32]], axis=-1)
    turned = rotary * factors[:, :64] + swapped * factors[:, 64:]
    return jnp.concatenate([scaled, turned], axis=-1).astype(bf16)


def dense_keys(every, place, embed_table, down, latent_gain, cache_length):
    group = place[0] * 8 + place[1]
    tp_index = place[2] * 2 + place[3]
    local_row = every.reshape(-1) - (group * 2 + place[4]) * 2048
    inside = (local_row >= 0) & (local_row < 2048)
    picked = jnp.take(embed_table, jnp.clip(local_row, 0, 2047), axis=0)
    picked = jnp.where(inside[:, None], picked, jnp.zeros_like(picked)).reshape(32, 128, 896)
    embedded = jnp.sum(lax.all_to_all(picked, HOLDERS, 0, 0, tiled=True).astype(f32), axis=0).astype(bf16)
    partial = dot_nt(embedded, down)
    spread = jnp.broadcast_to(partial[None], (8, 128, KVW))
    latent = jnp.sum(lax.all_to_all(spread, TP, 0, 0, tiled=True), axis=0)
    index = jnp.arange(128, dtype=jnp.int32)
    mine = finish_keys(latent, latent_gain, group * 64 + index // 2)
    spread = jnp.broadcast_to(mine[None], (32, 128, KVW))
    prompts = lax.all_to_all(spread, HOLDERS, 0, 0, tiled=True).reshape(16, 2, 64, 2, KVW)[:, 0]
    prompts = jnp.transpose(prompts, (2, 0, 1, 3)).reshape(KEYS, KVW)
    own = lax.dynamic_slice_in_dim(latent, tp_index * 16, 16, 0)
    fresh = finish_keys(own, latent_gain, (cache_length[:, None] + jnp.arange(2, dtype=jnp.int32)[None]).reshape(-1))
    return prompts, jnp.concatenate([fresh, jnp.zeros((112, KVW), bf16)], axis=0)


def params(mebibytes):
    return pltpu.CompilerParams(vmem_limit_bytes=mebibytes * 1024 * 1024)


def cache_attention(cache_length, decode_query, latent_cache):
    return pl.pallas_call(
        cache_kernel,
        grid_spec=pltpu.PrefetchScalarGridSpec(
            num_scalar_prefetch=1,
            grid=(8,),
            in_specs=[
                pl.BlockSpec((1, 128, KVW), lambda row, lengths: (row, 0, 0)),
                pl.BlockSpec((1, KVW, 512), lambda row, lengths: (row, 0, 0)),
            ],
            out_specs=[
                pl.BlockSpec((128, LAT), lambda row, lengths: (row, 0)),
                pl.BlockSpec((128, 128), lambda row, lengths: (row, 0)),
            ],
        ),
        out_shape=(jax.ShapeDtypeStruct((1024, LAT), bf16), jax.ShapeDtypeStruct((1024, 128), f32)),
        compiler_params=params(12),
        cost_estimate=pl.CostEstimate(flops=12 * 10**8, bytes_accessed=7 * 10**6, transcendentals=524288),
        name="cache_rows",
    )(cache_length, decode_query.reshape(8, 128, KVW), jnp.swapaxes(latent_cache, 1, 2))


def shards(
    token_ids,
    embed_table,
    latent_down,
    latent_gain,
    prefill_query,
    decode_query,
    latent_cache,
    cache_length,
    prompt_owner,
):
    place = jnp.stack([lax.axis_index(name) for name in ("ylo", "z", "x", "core", "role")]).astype(jnp.int32)
    section = place[4]
    group = place[0] * 8 + place[1]
    down = jnp.transpose(latent_down)
    whole = pl.BlockSpec(memory_space=VMEM)
    scalars = pl.BlockSpec(memory_space=SMEM)
    anywhere = pl.BlockSpec(memory_space=pl.ANY)

    every = lax.all_to_all(jnp.broadcast_to(token_ids, (32, 128)).reshape(32, 1, 128), HOLDERS, 0, 0, tiled=True)
    every = every.reshape(32, 128)
    earlier, level = cache_attention(cache_length, decode_query, latent_cache)
    every, earlier, level = lax.optimization_barrier((every, earlier, level))

    partial = pl.pallas_call(
        select_kernel,
        out_shape=jax.ShapeDtypeStruct((8, SLOTS, KVW), f32),
        in_specs=[scalars, whole, anywhere, anywhere],
        out_specs=whole,
        scratch_shapes=[
            VMEM((16, 4096), bf16),
            VMEM((128, 4096), bf16),
            VMEM((8 * SLOTS, 2048), bf16),
            VMEM((2048, 896), bf16),
            VMEM((KVW, 896), bf16),
            pltpu.SemaphoreType.DMA((2,)),
        ],
        compiler_params=params(16),
        cost_estimate=pl.CostEstimate(flops=3 * 10**9, bytes_accessed=5 * 10**6, transcendentals=0),
        name="select_rows",
    )((group * 2 + section).reshape(1), every, embed_table, down)
    parts = lax.all_to_all(partial, TP, 0, 0, tiled=True)

    columns, kept, fits = pl.pallas_call(
        place_kernel,
        out_shape=(
            jax.ShapeDtypeStruct((128, 128), jnp.int32),
            jax.ShapeDtypeStruct((8, 128), f32),
            jax.ShapeDtypeStruct((1, 1), jnp.int32),
        ),
        in_specs=[scalars, whole],
        out_specs=(whole, whole, scalars),
        scratch_shapes=[
            VMEM((512, 4096), bf16),
            VMEM((128, 4096), bf16),
            VMEM((128, 19 * 128), bf16),
            VMEM((128, 19 * 128), bf16),
            VMEM((96, 128), jnp.int32),
            VMEM((128, 128), f32),
        ],
        compiler_params=params(20),
        cost_estimate=pl.CostEstimate(flops=3 * 10**9, bytes_accessed=10**6, transcendentals=0),
        name="place_rows",
    )(place, every)

    parts, columns, kept, fits = lax.optimization_barrier((parts, columns, kept, fits))
    sent = pl.pallas_call(
        finish_kernel,
        out_shape=jax.ShapeDtypeStruct((8, SLOTS, WIDE), bf16),
        in_specs=[whole, whole],
        out_specs=whole,
        compiler_params=params(8),
        name="finish_rows",
    )(parts, latent_gain.reshape(1, LAT))
    arrived = lax.all_to_all(sent, "z", 0, 0, tiled=True)
    handed = pl.pallas_call(
        keep_kernel,
        out_shape=jax.ShapeDtypeStruct((16, KEPT, WIDE), bf16),
        in_specs=[whole, whole],
        out_specs=whole,
        compiler_params=params(8),
        name="keep_rows",
    )(kept, arrived.reshape(8 * SLOTS, WIDE))
    slots = lax.all_to_all(handed, PLANE, 0, 0, tiled=True).reshape(SIDE, WIDE)
    prompt_query = jnp.transpose(prefill_query.reshape(64, 2, 8, KVW), (1, 2, 0, 3)).reshape(1024, KVW)
    new_position = (cache_length[:, None] + jnp.arange(2, dtype=jnp.int32)[None]).reshape(-1)
    new_factors = jnp.pad(rope_factors(new_position.astype(f32)), ((0, 112), (0, 0)))
    slots, prompt_query, new_factors = lax.optimization_barrier((slots, prompt_query, new_factors))
    others = lax.ppermute(slots, "core", [(0, 1), (1, 0)])

    spare, spare_new = lax.cond(
        fits[0, 0] == 1,
        lambda *unused: (jnp.zeros((KEYS, KVW), bf16), jnp.zeros((128, KVW), bf16)),
        dense_keys,
        every,
        place,
        embed_table,
        down,
        latent_gain,
        cache_length,
    )
    near = pl.pallas_call(
        near_kernel,
        out_shape=jax.ShapeDtypeStruct((KEYS + 128, WIDE), bf16),
        in_specs=[scalars, scalars, whole, whole],
        out_specs=whole,
        scratch_shapes=[VMEM((1024, SIDE), bf16)],
        compiler_params=params(16),
        cost_estimate=pl.CostEstimate(flops=2 * 10**9, bytes_accessed=10**6, transcendentals=0),
        name="near_keys",
    )(place, prompt_owner, slots, columns)
    factors = jnp.asarray(rope_factors(np.arange(1024, dtype=np.float32)))
    decoded = pl.pallas_call(
        decode_kernel,
        out_shape=jax.ShapeDtypeStruct((128, 4096), bf16),
        in_specs=[scalars] * 3 + [whole] * 8 + [anywhere] * 2,
        out_specs=whole,
        scratch_shapes=[
            VMEM((KEYS + 128, KVW), bf16),
            VMEM((1024, SIDE), bf16),
            VMEM((1024, 128), f32),
            VMEM((1024, 128), f32),
            VMEM((1024, LAT), f32),
            VMEM((4, 1024, 128), f32),
            pltpu.SemaphoreType.DMA,
        ],
        compiler_params=params(28),
        cost_estimate=pl.CostEstimate(flops=5 * 10**9, bytes_accessed=7 * 10**6, transcendentals=10**6),
        name="decode_rows",
    )(
        place, prompt_owner, fits, near, others, columns, factors, new_factors, decode_query.reshape(1024, KVW),
        earlier, level, spare, spare_new,
    )
    turned = lax.all_to_all(decoded.reshape(8, 16, 4096), TP, 0, 0, tiled=True).reshape(128, 4096)
    prefilled = pl.pallas_call(
        prefill_kernel,
        out_shape=jax.ShapeDtypeStruct((128, 4096), bf16),
        in_specs=[scalars] * 2 + [whole] * 5 + [anywhere],
        out_specs=whole,
        scratch_shapes=[
            VMEM((1024, KVW), bf16),
            VMEM((1024, SIDE), bf16),
            VMEM((1024, 128), f32),
            VMEM((1024, 128), f32),
            VMEM((1024, LAT), f32),
            VMEM((1024, WIDE), f32),
            pltpu.SemaphoreType.DMA,
        ],
        compiler_params=params(28),
        cost_estimate=pl.CostEstimate(flops=7 * 10**9, bytes_accessed=7 * 10**6, transcendentals=10**6),
        name="prefill_rows",
    )(place, fits, slots, others, columns, factors, prompt_query, spare)
    return jnp.where(section == 0, prefilled, turned)[None]


def solution(mesh):
    fine_mesh = Mesh(mesh.devices.reshape(2, 8, 4, 2, 2), ("ylo", "z", "x", "core", "role"))
    ctx, tp = ("ylo", "z"), ("x", "core")
    in_specs = (
        P("role", ctx),
        P(ctx + ("role",), tp),
        P(tp, None),
        P(),
        P(ctx, tp, None),
        P(ctx + tp, None, None, None),
        P(ctx + tp, None, None),
        P(ctx + tp),
        P(),
    )
    out_specs = P("role", ctx, tp)
    return jax.shard_map(shards, mesh=fine_mesh, in_specs=in_specs, out_specs=out_specs, check_vma=False)
```

time: 552 us -> 120 us (0.22)
  the two profiles are of different devices: /device:TPU:88 before, /device:TPU:56 now
where the time goes in v1:
time: 120 us
  Pallas kernels  38 us (32%)
  starting transfers between devices  26.9 us (22%)
  waiting for transfers between devices  22.1 us (18%)
  blocking collectives  16.2 us (14%)
  local copies, waits for them, and re-layouts  13.6 us (11%)
  other arithmetic  2.56 us (2%)
    all_to_all x1, blocking collectives, shards(): arrived = lax.all_to_all(sent, 'z', 0, 0, tiled=True)  16.2 us
    pallas_call x1, Pallas kernels, shards(): pl.pallas_call(decode_kernel, out_shape=jax.ShapeDtypeStruct((128, 4096),...  14.3 us
    all_to_all x1, waiting for transfers between devices, shards(): lax.all_to_all(decoded.reshape(8, 16, 4096), TP, 0, 0, tiled=True)  12.6 us
    all_to_all x1, starting transfers between devices, shards(): lax.all_to_all(jnp.broadcast_to(token_ids, (32, 128)).reshape(32, 1, 128)...  11 us
    unnamed x37, local copies, waits for them, and re-layouts  9.72 us
    all_to_all x1, waiting for transfers between devices, shards(): slots = lax.all_to_all(handed, PLANE, 0, 0, tiled=True).reshape(SIDE, WIDE)  9.46 us
    pallas_call x1, Pallas kernels, shards(): pl.pallas_call(place_kernel, out_shape=(jax.ShapeDtypeStruct((128, 128),...  8.89 us
    all_to_all x1, starting transfers between devices, shards(): slots = lax.all_to_all(handed, PLANE, 0, 0, tiled=True).reshape(SIDE, WIDE)  7.28 us
  transfers between devices with their start and end apart: 5, of which 2 were waited for; matrix products, arithmetic and copies ran while one was open for 4% of the time, Pallas kernels for 15%

profile of v1, /device:TPU:56, one launch (start us, length us, event | category | flops | bytes accessed | tf_op | source)
XLA Modules:
  0.0 120.4 jit_solution(2494174604434594796)
XLA Ops:
  0.0 1.3 %reshape.177 = s32[32,1,128]{2,1,0:T(1,128)} broadcast(s32[128]{0:T(128)} %bitcast.55), dimensions={2} | broadcast | bytes 16896 | tf_op jit(solution)/shard_map/reshape | solution.py:543
  1.3 11.0 %all-to-all-start.3 = ((s32[32,1,128]{2,1,0:T(1,128)}), s32[32,1,128]{2,1,0:T(1,128)S(1)}, u32[]{:S(2)}, u32[]{:S(2)}) async-start(s32[32,1,128]{2,1,0:T(1,128)} %reshape.177), calls=%async_computation.3 | async-start | bytes 32768 | tf_op jit(solution)/shard_map/all_to_all | solution.py:543
  12.3 2.3 %copy-done = bf16[8,512,576]{1,2,0:T(8,128)(2,1)S(1)} copy-done((bf16[8,512,576]{1,2,0:T(8,128)(2,1)S(1)}, bf16[8,512,576]{1,2,0:T(8,128)(2,1)}, u32[]{:S(2)}) %copy-start) | copy-done | bytes 4718616
  14.6 1.3 %copy-done.1 = bf16[8,2,64,576]{3,2,1,0:T(8,128)(2,1)S(1)} copy-done((bf16[8,2,64,576]{3,2,1,0:T(8,128)(2,1)S(1)}, bf16[8,2,64,576]{3,2,1,0:T(8,128)(2,1)}, u32[]{:S(2)}) %copy-start.1) | copy-done | bytes 1179672
  16.0 5.3 %cache_rows.1 = (bf16[1024,512]{1,0:T(8,128)(2,1)S(1)}, f32[1024,128]{1,0:T(8,128)S(1)}) custom-call(s32[8]{0:T(128)} %lengths.1, bf16[8,128,576]{2,1,0:T(8,128)(2,1)S(1)} %bitcast.38, bf16[8,576,512]{2,1,0:T(8,128)(2,1)S(1)} %bitcast.36), custom_call_target="tpu_custom_call" | custom-call | flops 1200000000 | bytes 7000000 | tf_op jit(solution)/shard_map/cache_rows/pallas_call | solution.py:503
  21.3 1.0 copy-done.3
  22.3 0.8 copy-done.7
  23.1 0.1 stack.23.place
  23.2 4.0 %select_rows.1 = f32[8,16,576]{2,1,0:T(8,128)} custom-call(s32[1]{0:T(128)} %bitcast.13.place, s32[32,128]{1,0:T(8,128)S(1)} %bitcast.50, bf16[2048,896]{1,0:T(8,128)(2,1)} %table.1, bf16[576,896]{1,0:T(8,128)(2,1)} %bitcast.47), custom_call_target="tpu_custom_call" | custom-call | flops 3000000000 | bytes 5000000 | tf_op jit(solution)/shard_map/select_rows/pallas_call | solution.py:548
  27.2 4.3 %all-to-all-start.4 = ((f32[8,16,576]{2,1,0:T(8,128)}), f32[8,16,576]{2,1,0:T(8,128)S(1)}, u32[]{:S(2)}, u32[]{:S(2)}) async-start(f32[8,16,576]{2,1,0:T(8,128)} %select_rows.1), calls=%async_computation.4 | async-start | bytes 655360 | tf_op jit(solution)/shard_map/all_to_all | solution.py:565
  31.5 8.9 %place_rows.1 = (s32[128,128]{1,0:T(8,128)S(1)}, f32[8,128]{1,0:T(8,128)S(1)}, s32[1,1]{1,0:T(1,128)}) custom-call(s32[5]{0:T(128)S(1)} %stack.23.place, s32[32,128]{1,0:T(8,128)S(1)} %bitcast.51), custom_call_target="tpu_custom_call" | custom-call | flops 3000000000 | bytes 1000000 | tf_op jit(solution)/shard_map/place_rows/pallas_call | solution.py:567
  40.5 0.1 finish_rows.1
  40.6 16.2 %all_to_all.38 = bf16[8,16,640]{2,1,0:T(8,128)(2,1)S(1)} all-to-all(bf16[8,16,640]{2,1,0:T(8,128)(2,1)S(1)} %finish_rows.1), channel_id=1, replica_groups=mesh['ylo'=2,'z'=8,'x'=4,'core'=2,'role'=2] {'z'}, dimensions={0} | all-to-all | bytes 327680 | tf_op jit(solution)/shard_map/all_to_all | solution.py:598
  56.8 1.2 keep_rows.1
  57.9 7.3 %all-to-all-start.6 = ((bf16[16,48,640]{2,1,0:T(8,128)(2,1)}), bf16[16,48,640]{2,1,0:T(8,128)(2,1)S(1)}, u32[]{:S(2)}, u32[]{:S(2)}) async-start(bf16[16,48,640]{2,1,0:T(8,128)(2,1)} %keep_rows.1), calls=%async_computation.6 | async-start | bytes 1966080 | tf_op jit(solution)/shard_map/all_to_all | solution.py:607
  65.2 2.0 %copy.59 = bf16[128,8,576]{2,1,0:T(8,128)(2,1)} copy(bf16[128,8,576]{0,2,1:T(8,128)(2,1)S(1)} %copy-done.13) | data formatting | bytes 2359296 | tf_op args[4]
  67.2 1.6 %copy.60 = bf16[2,8,64,576]{3,2,1,0:T(8,128)(2,1)S(1)} copy(bf16[2,8,64,576]{3,1,0,2:T(8,128)(2,1)} %bitcast.45) | data formatting | bytes 2359296 | tf_op jit(solution)/shard_map/transpose | solution.py:608
  68.9 0.1 convert_element_type.44
  69.0 0.1 multiply_cosine_fusion.2
  69.1 0.1 select_maximum_fusion.new_factors
  69.2 9.5 %all-to-all-done.6 = bf16[16,48,640]{2,1,0:T(8,128)(2,1)S(1)} async-done(((bf16[16,48,640]{2,1,0:T(8,128)(2,1)}), bf16[16,48,640]{2,1,0:T(8,128)(2,1)S(1)}, u32[]{:S(2)}, u32[]{:S(2)}) %all-to-all-start.6) | async-done | bytes 983072 | tf_op jit(solution)/shard_map/all_to_all | solution.py:607
  79.2 1.1 conditional.1
  79.5 0.2 broadcast.177
  79.7 0.7 broadcast.178
  80.4 3.0 %near_keys.1.near = bf16[2176,640]{1,0:T(8,128)(2,1)S(1)} custom-call(s32[5]{0:T(128)S(1)} %stack.23.place, s32[2]{0:T(128)S(1)} %copy-done.9, bf16[768,640]{1,0:T(8,128)(2,1)S(1)} %bitcast.41, s32[128,128]{1,0:T(8,128)S(1)} %get-tuple-element.68.columns), custom_call_target="tpu_custom_call" | custom-call | flops 2000000000 | bytes 1000000 | tf_op jit(solution)/shard_map/near_keys/pallas_call | solution.py:625
  83.5 14.3 %decode_rows.1 = bf16[128,4096]{1,0:T(8,128)(2,1)} custom-call(s32[5]{0:T(128)S(1)} %stack.23.place, s32[2]{0:T(128)S(1)} %copy-done.9, s32[1,1]{1,0:T(1,128)} %get-tuple-element.64.fits, bf16[2176,640]{1,0:T(8,128)(2,1)S(1)} %near_keys.1.near, bf16[768,640]{1,0:T(8,128)(2,1)S(1)} %collective-permute-done.others, s32[128,128]{1,0:T(8,128)S(1)} %get-tuple-element.68.columns, ...), custom_call_target="tpu_custom_call" | custom-call | flops 5000000000 | bytes 7000000 | tf_op jit(solution)/shard_map/decode_rows/pallas_call | solution.py:636
  97.9 4.3 %all-to-all-start.7 = ((bf16[8,16,4096]{2,1,0:T(8,128)(2,1)}), bf16[8,16,4096]{2,1,0:T(8,128)(2,1)}, u32[]{:S(2)}, u32[]{:S(2)}) async-start(bf16[8,16,4096]{2,1,0:T(8,128)(2,1)} %bitcast.27), calls=%async_computation.7 | async-start | bytes 2097152 | tf_op jit(solution)/shard_map/all_to_all | solution.py:657
  102.2 1.2 copy-done.6
  103.4 1.0 copy-done.11
  104.4 1.1 prefill_rows.1
  105.6 12.6 %all-to-all-done.7 = bf16[8,16,4096]{2,1,0:T(8,128)(2,1)} async-done(((bf16[8,16,4096]{2,1,0:T(8,128)(2,1)}), bf16[8,16,4096]{2,1,0:T(8,128)(2,1)}, u32[]{:S(2)}, u32[]{:S(2)}) %all-to-all-start.7) | async-done | bytes 1048608 | tf_op jit(solution)/shard_map/all_to_all | solution.py:657
  118.1 2.3 %bitcast_select_fusion = bf16[128,4096]{1,0:T(8,128)(2,1)} fusion(bf16[128,4096]{1,0:T(8,128)(2,1)S(1)} %prefill_rows.1, bf16[8,16,4096]{2,1,0:T(8,128)(2,1)} %all-to-all-done.7, pred[]{:T(512)S(6)} %eq.7), kind=kLoop, calls=%fused_computation.42 | loop fusion | flops 524288 | bytes 3145729 | tf_op jit(solution)/shard_map/jit(_where)/select_n | solution.py:676
  (35 shorter events, 0.2 us)
Async XLA Ops:
  1.3 21.9 %all-to-all-start.3 = ((s32[32,1,128]{2,1,0:T(1,128)}), s32[32,1,128]{2,1,0:T(1,128)S(1)}, u32[]{:S(2)}, u32[]{:S(2)}) async-start(s32[32,1,128]{2,1,0:T(1,128)} %reshape.177), calls=%async_computation.3 | async-start | bytes 32768 | tf_op jit(solution)/shard_map/all_to_all | solution.py:543
  12.3 2.3 %copy-start = (bf16[8,512,576]{1,2,0:T(8,128)(2,1)S(1)}, bf16[8,512,576]{1,2,0:T(8,128)(2,1)}, u32[]{:S(2)}) copy-start(bf16[8,512,576]{1,2,0:T(8,128)(2,1)} %param.21) | copy-start | bytes 14155780
  14.6 1.3 %copy-start.1 = (bf16[8,2,64,576]{3,2,1,0:T(8,128)(2,1)S(1)}, bf16[8,2,64,576]{3,2,1,0:T(8,128)(2,1)}, u32[]{:S(2)}) copy-start(bf16[8,2,64,576]{3,2,1,0:T(8,128)(2,1)} %param.20) | copy-start | bytes 3538948
  21.3 1.0 copy-start.3
  22.3 0.8 copy-start.7
  27.2 13.3 %all-to-all-start.4 = ((f32[8,16,576]{2,1,0:T(8,128)}), f32[8,16,576]{2,1,0:T(8,128)S(1)}, u32[]{:S(2)}, u32[]{:S(2)}) async-start(f32[8,16,576]{2,1,0:T(8,128)} %select_rows.1), calls=%async_computation.4 | async-start | bytes 655360 | tf_op jit(solution)/shard_map/all_to_all | solution.py:565
  31.5 9.0 %copy-start.15 = (f32[512]{0:T(512)S(1)}, f32[512]{0:T(512)}, u32[]{:S(2)}) copy-start(f32[512]{0:T(512)} %param.18) | copy-start | bytes 6148
  40.4 24.8 %copy-start.13 = (bf16[128,8,576]{0,2,1:T(8,128)(2,1)S(1)}, bf16[128,8,576]{0,2,1:T(8,128)(2,1)}, u32[]{:S(2)}) copy-start(bf16[128,8,576]{0,2,1:T(8,128)(2,1)} %param.19) | copy-start | bytes 3538948
  40.4 28.4 %copy-start.16 = (s32[8]{0:T(128)S(1)}, s32[8]{0:T(128)}, u32[]{:S(2)}) copy-start(s32[8]{0:T(128)} %lengths.1) | copy-start | bytes 100
  40.5 28.5 %copy-start.18 = (f32[32]{0:T(128)S(1)}, f32[32]{0:T(128)}, u32[]{:S(2)}) copy-start(f32[32]{0:T(128)} %constant.107) | copy-start | bytes 388
  57.9 20.7 %all-to-all-start.6 = ((bf16[16,48,640]{2,1,0:T(8,128)(2,1)}), bf16[16,48,640]{2,1,0:T(8,128)(2,1)S(1)}, u32[]{:S(2)}, u32[]{:S(2)}) async-start(bf16[16,48,640]{2,1,0:T(8,128)(2,1)} %keep_rows.1), calls=%async_computation.6 | async-start | bytes 1966080 | tf_op jit(solution)/shard_map/all_to_all | solution.py:607
  78.7 4.8 %collective-permute-start = (bf16[768,640]{1,0:T(8,128)(2,1)S(1)}, bf16[768,640]{1,0:T(8,128)(2,1)S(1)}, u32[]{:S(2)}, u32[]{:S(2)}) collective-permute-start(bf16[768,640]{1,0:T(8,128)(2,1)S(1)} %bitcast.40), channel_id=1, source_target_pairs={{0,2},{2,0},{1,3},{3,1},{4,6},{6,4},{5,7},{7,5},{8,10},{10,8},{9,1... | collective-permute-start | bytes 2949128 | tf_op jit(solution)/shard_map/ppermute | solution.py:612
  79.2 1.1 copy-start.9
  80.4 3.1 %copy-start.12 = (bf16[2048,576]{1,0:T(8,128)(2,1)}, bf16[2048,576]{1,0:T(8,128)(2,1)S(1)}, u32[]{:S(2)}) copy-start(bf16[2048,576]{1,0:T(8,128)(2,1)S(1)} %get-tuple-element.70.spare) | copy-start | bytes 7077892
  80.4 3.1 %copy-start.2 = (bf16[8,2,64,576]{3,2,1,0:T(8,128)(2,1)S(1)}, bf16[8,2,64,576]{3,2,1,0:T(8,128)(2,1)}, u32[]{:S(2)}) copy-start(bf16[8,2,64,576]{3,2,1,0:T(8,128)(2,1)} %param.20) | copy-start | bytes 3538948
  80.4 3.1 %copy-start.4 = (bf16[1024,512]{1,0:T(8,128)(2,1)S(1)}, bf16[1024,512]{1,0:T(8,128)(2,1)}, u32[]{:S(2)}) copy-start(bf16[1024,512]{1,0:T(8,128)(2,1)} %copy-done.3) | copy-start | bytes 3145732
  80.4 3.1 %copy-start.8 = (f32[1024,128]{1,0:T(8,128)S(1)}, f32[1024,128]{1,0:T(8,128)}, u32[]{:S(2)}) copy-start(f32[1024,128]{1,0:T(8,128)} %copy-done.7) | copy-start | bytes 1572868
  80.4 3.1 %copy-start.10 = (f32[1024,128]{1,0:T(8,128)S(1)}, f32[1024,128]{1,0:T(8,128)}, u32[]{:S(2)}) copy-start(f32[1024,128]{1,0:T(8,128)} %constant.98.clone.factors) | copy-start | bytes 1572868
  80.4 3.1 %copy-start.14 = (bf16[128,576]{1,0:T(8,128)(2,1)S(1)}, bf16[128,576]{1,0:T(8,128)(2,1)}, u32[]{:S(2)}) copy-start(bf16[128,576]{1,0:T(8,128)(2,1)} %get-tuple-element.74.spare_new) | copy-start | bytes 442372
  83.5 14.4 %copy-start.5 = (bf16[768,640]{1,0:T(8,128)(2,1)}, bf16[768,640]{1,0:T(8,128)(2,1)S(1)}, u32[]{:S(2)}) copy-start(bf16[768,640]{1,0:T(8,128)(2,1)S(1)} %collective-permute-done.others) | copy-start | bytes 2949124
  97.9 20.2 %all-to-all-start.7 = ((bf16[8,16,4096]{2,1,0:T(8,128)(2,1)}), bf16[8,16,4096]{2,1,0:T(8,128)(2,1)}, u32[]{:S(2)}, u32[]{:S(2)}) async-start(bf16[8,16,4096]{2,1,0:T(8,128)(2,1)} %bitcast.27), calls=%async_computation.7 | async-start | bytes 2097152 | tf_op jit(solution)/shard_map/all_to_all | solution.py:657
  102.2 1.2 copy-start.6
  103.4 1.0 copy-start.11
